TPU v7x, 32 devices: a whole 2x2x4 slice. The times are simulated.
32 devices in a mesh: section: 2 (over x), ep: 16 (over z, y, core).
Axes of the slice: x: 2, y: 2, z: 4, core: 2. Of those that a mesh axis runs over, the one named last changes fastest.
Arguments:
- hidden_in: bfloat16 [2, 128, 4096], P('section', 'ep'), may hold values from -6 to 6
- query: bfloat16 [2, 2, 128, 8192], P('section', None, 'ep'), may hold values from -60 to 60
- new_kv: bfloat16 [2, 2, 128, 1024], P('section', None, 'ep'), may hold values from -4 to 4
- kv_cache: bfloat16 [2, 2, 128, 128, 1024], P('section', None, 'ep'), may hold values from -4 to 4
- lengths: int32 [2, 128], P(None, 'ep'), may hold values from 2 to 128, as said below
- out_proj: bfloat16 [2, 8192, 4096], P('section', 'ep'), may hold values from -0.25 to 0.25
- norm_gain: float32 [2, 4096], P('section'), may hold values from 0.1 to 1.9
- w_gate_up: bfloat16 [2, 16, 4096, 1536], P('section', 'ep'), may hold values from -0.09375 to 0.09375
- w_down: bfloat16 [2, 16, 768, 4096], P('section', 'ep'), may hold values from -0.21875 to 0.21875
- expert_ids: int32 [2, 2, 128, 8], P('section'), may hold values from 0 to 15, all different within a row; in each aligned block of 8 rows (0 to 7, 8 to 15, ..., all dimensions but the last counted through in order) at most 8 rows name the same one
- route_weight: float32 [2, 2, 128, 8], P('section', None, 'ep'), may hold values from 0.05 to 1
Outputs:
- finished: bfloat16 [2, 128, 4096], P('section', 'ep')
Inputs may be any that keep to these rules, and one draw needn't show every extreme that they name: `expert_ids`: each row names 8 different experts; among the rows of one index of ep of one micro-batch no expert is named by more than 8 rows, and that bound is reached. `lengths`: row 0 of micro-batch 0 uses all 128 positions.
All inputs are finite; a program needn't handle non-finite values.
Results may differ from a plain program's by a relative error of at most 0.0075.
Values may be sent and summed in bfloat16 or wider, within the bound.
A program may use at most 128 MiB of HBM per device.

v0:
```python
import math

import jax
import jax.numpy as jnp
from jax import lax
from jax.sharding import PartitionSpec as P

HEADS = 64
KVH = 4
HD = 128


def passed_along(array, axis, by):
    peers = lax.axis_size(axis)
    return lax.ppermute(array, axis, [(i, (i + by) % peers) for i in range(peers)])


def slot_numbers(picks, count):
    flat = picks.reshape(picks.shape[:-2] + (-1,))
    onehot = (flat[..., None] == jnp.arange(count, dtype=jnp.int32)).astype(jnp.int32)
    earlier = jnp.cumsum(onehot, axis=-2) - onehot
    return jnp.sum(onehot * earlier, axis=-1).reshape(picks.shape)


def attend(query, cache, newest, lengths):
    rows = query.shape[0]
    positions = cache.shape[1]
    group = HEADS // KVH
    scale = 1.0 / math.sqrt(HD)
    q_heads = query.reshape(rows, KVH, group, HD)
    keys = cache[..., : KVH * HD].reshape(rows, positions, KVH, HD)
    values = cache[..., KVH * HD :].reshape(rows, positions, KVH, HD)
    new_keys = newest[:, : KVH * HD].reshape(rows, KVH, HD)
    new_values = newest[:, KVH * HD :].reshape(rows, KVH, HD)
    scores = (
        jnp.einsum("rgqd,rpgd->rgqp", q_heads, keys, preferred_element_type=jnp.float32) * scale
    )
    fresh = (
        jnp.einsum("rgqd,rgd->rgq", q_heads, new_keys, preferred_element_type=jnp.float32) * scale
    )
    valid = (jnp.arange(positions, dtype=jnp.int32)[None, :] < lengths[:, None])[:, None, None, :]
    top = jnp.maximum(jnp.max(jnp.where(valid, scores, -jnp.inf), axis=-1), fresh)
    expo = jnp.where(valid, jnp.exp(scores - top[..., None]), 0.0)
    expo_new = jnp.exp(fresh - top)
    total = jnp.sum(expo, axis=-1) + expo_new
    probs = (expo / total[..., None]).astype(jnp.bfloat16)
    probs_new = (expo_new / total).astype(jnp.bfloat16)
    mixed = jnp.einsum("rgqp,rpgd->rgqd", probs, values, preferred_element_type=jnp.float32)
    mixed = (
        mixed
        + probs_new.astype(jnp.float32)[..., None] * new_values.astype(jnp.float32)[:, :, None, :]
    )
    return mixed.reshape(rows, HEADS * HD).astype(jnp.bfloat16)


def expert_outputs(slots, w_pair, w_out):
    width = w_out.shape[0]
    act = jnp.einsum("scd,df->scf", slots, w_pair, preferred_element_type=jnp.float32)
    units = (jax.nn.silu(act[..., :width]) * act[..., width:]).astype(jnp.bfloat16)
    return jnp.einsum("scf,fd->scd", units, w_out, preferred_element_type=jnp.float32).astype(
        jnp.bfloat16
    )


def send_back(results):
    return lax.all_to_all(results, "ep", split_axis=0, concat_axis=0, tiled=True)


def layer_apply(
    hidden, query, newest, cache, lengths, proj_rows, gain, w_pair, w_out, picks_all, weights
):
    rows = hidden.shape[0]
    groups = lax.axis_size("ep")
    member = lax.axis_index("ep")
    topk = picks_all.shape[-1]
    capacity = max(2, 2 * rows * topk // groups)
    attn = attend(query, cache, newest, lengths)
    head_rows = lax.all_to_all(attn, "ep", split_axis=1, concat_axis=0, tiled=True)
    summed = lax.psum_scatter(
        jnp.dot(head_rows, proj_rows, preferred_element_type=jnp.float32),
        "ep",
        scatter_dimension=0,
        tiled=True,
    )
    h_att = hidden.astype(jnp.float32) + summed
    meansq = jnp.mean(h_att * h_att, axis=-1, keepdims=True)
    x_rows = (h_att * lax.rsqrt(meansq + 1e-06) * gain[None, :]).astype(jnp.bfloat16)
    picks_mine = lax.dynamic_slice_in_dim(picks_all, member * rows, rows, 0)
    slots_mine = slot_numbers(picks_mine, groups)
    match_expert = (picks_mine[..., None] == jnp.arange(groups, dtype=jnp.int32)).astype(
        jnp.bfloat16
    )
    match_slot = (slots_mine[..., None] == jnp.arange(capacity, dtype=jnp.int32)).astype(
        jnp.bfloat16
    )
    select = jnp.einsum(
        "rke,rkc->ecr", match_expert, match_slot, preferred_element_type=jnp.float32
    ).astype(jnp.bfloat16)
    outgoing = jnp.einsum("ecr,rd->ecd", select, x_rows, preferred_element_type=jnp.float32).astype(
        jnp.bfloat16
    )
    returned = send_back(
        expert_outputs(
            lax.all_to_all(outgoing, "ep", split_axis=0, concat_axis=0, tiled=True), w_pair, w_out
        )
    )
    placing = match_expert[..., :, None] * match_slot[..., None, :]
    chosen = jnp.einsum("rkec,ecd->rkd", placing, returned, preferred_element_type=jnp.float32)
    share = weights / jnp.sum(weights, axis=-1, keepdims=True)
    moe = jnp.sum(share[..., None] * chosen, axis=1)
    return (h_att + moe).astype(jnp.bfloat16)


def on_device(
    hidden_in,
    query,
    new_kv,
    kv_cache,
    lengths,
    out_proj,
    norm_gain,
    w_gate_up,
    w_down,
    expert_ids,
    route_weight,
):
    sections = lax.axis_size("section")
    position = lax.axis_index("section")
    hidden = hidden_in[0]
    for tick in range(sections):
        micro = (position - tick) % sections
        hidden = layer_apply(
            hidden,
            lax.dynamic_index_in_dim(query[0], micro, 0, keepdims=False),
            lax.dynamic_index_in_dim(new_kv[0], micro, 0, keepdims=False),
            lax.dynamic_index_in_dim(kv_cache[0], micro, 0, keepdims=False),
            lax.dynamic_index_in_dim(lengths, micro, 0, keepdims=False),
            out_proj[0],
            norm_gain[0],
            w_gate_up[0, 0],
            w_down[0, 0],
            lax.dynamic_index_in_dim(expert_ids[0], micro, 0, keepdims=False),
            lax.dynamic_index_in_dim(route_weight[0], micro, 0, keepdims=False),
        )
        if tick + 1 < sections:
            hidden = passed_along(hidden, "section", 1)
    return hidden[None]


def solution(mesh):
    in_specs = (
        P("section", "ep", None),
        P("section", None, "ep", None),
        P("section", None, "ep", None),
        P("section", None, "ep", None, None),
        P(None, "ep"),
        P("section", "ep", None),
        P("section", None),
        P("section", "ep", None, None),
        P("section", "ep", None, None),
        P("section", None, None, None),
        P("section", None, "ep", None),
    )
    out_specs = P("section", "ep", None)
    return jax.shard_map(
        on_device, mesh=mesh, in_specs=in_specs, out_specs=out_specs, check_vma=False
    )
```

profile of v0, /device:TPU:0, one launch (start us, length us, event | category | flops | bytes accessed | tf_op | source)
XLA Modules:
  0.0 299.9 jit_solution(3076253086126150982)
XLA Ops:
  6.5 4.2 %constant_dynamic-slice_fusion.4 = (bf16[1,1,8,128,1024]{4,3,2,1,0:T(8,128)(2,1)}, bf16[1,1,8,128,1024]{4,3,2,1,0:T(8,128)(2,1)S(1)}) fusion(bf16[1,2,8,128,1024]{4,3,2,1,0:T(8,128)(2,1)} %param.14, s32[]{:T(128)S(6)} %select_n.57, s32[]{:T(128)S(6)} %select_n.64), kind=kLoop, calls=%fused_computation.129 | loop fusion | bytes 8388616 | tf_op jit(solution)/shard_map/jit(dynamic_index_in_dim)/dynamic_slice | solution.py:136
  10.8 3.9 %copy.24 = bf16[1,1,8,128,1024]{3,4,2,1,0:T(8,128)(2,1)} copy(bf16[1,1,8,128,1024]{4,3,2,1,0:T(8,128)(2,1)} %get-tuple-element.7) | data formatting | bytes 4194304 | tf_op jit(solution)/shard_map/jit(dynamic_index_in_dim)/dynamic_slice | solution.py:136
  14.7 1.7 fusion.83
  20.8 2.1 fusion.22
  24.0 15.1 %all_to_all.52 = bf16[8,16,512]{2,0,1:T(8,128)(2,1)S(1)} all-to-all(bf16[8,16,512]{2,0,1:T(8,128)(2,1)S(1)} %copy.27), channel_id=1, replica_groups=mesh['section'=2,'ep'=16] {'ep'}, dimensions={1} | all-to-all | bytes 262144 | tf_op jit(solution)/shard_map/all_to_all | solution.py:78
  39.1 4.3 %fusion.18 = f32[128,4096]{1,0:T(8,128)} fusion(bf16[1,512,4096]{2,1,0:T(8,128)(2,1)} %param.16, bf16[8,16,512]{2,0,1:T(8,128)(2,1)S(1)} %all_to_all.52), kind=kOutput, calls=%fused_computation.18 | convolution fusion | flops 536870912 | bytes 6422528 | tf_op jit(solution)/shard_map/dot_general | solution.py:80
  45.0 57.7 %reduce-scatter.3.cloned.1.call-done = f32[8,4096]{1,0:T(8,128)} async-done(((f32[128,4096]{1,0:T(8,128)}), f32[8,4096]{1,0:T(8,128)}) %reduce-scatter.3.cloned.1.call-update) | async-done | bytes 131088 | tf_op jit(solution)/shard_map/reduce_scatter | solution.py:79
  103.8 2.4 convolution_convert_fusion.1
  106.2 3.7 %all-to-all-start.1 = ((bf16[16,8,4096]{2,1,0:T(8,128)(2,1)}), bf16[16,8,4096]{2,1,0:T(8,128)(2,1)S(1)}, u32[]{:S(2)}, u32[]{:S(2)}) async-start(bf16[16,8,4096]{2,1,0:T(8,128)(2,1)} %convolution_convert_fusion.1), calls=%async_computation.2 | async-start | bytes 2097152 | tf_op jit(solution)/shard_map/all_to_all | solution.py:104
  109.9 2.4 copy.33
  112.6 1.7 fusion.84
  116.6 16.2 %all-to-all-done.1 = bf16[16,8,4096]{2,1,0:T(8,128)(2,1)S(1)} async-done(((bf16[16,8,4096]{2,1,0:T(8,128)(2,1)}), bf16[16,8,4096]{2,1,0:T(8,128)(2,1)S(1)}, u32[]{:S(2)}, u32[]{:S(2)}) %all-to-all-start.1) | async-done | bytes 1048608 | tf_op jit(solution)/shard_map/all_to_all | solution.py:104
  132.9 6.9 %all-to-all-start.3 = ((bf16[8,16,512]{2,0,1:T(8,128)(2,1)}), bf16[8,16,512]{2,0,1:T(8,128)(2,1)S(1)}, u32[]{:S(2)}, u32[]{:S(2)}) async-start(bf16[8,16,512]{2,0,1:T(8,128)(2,1)} %copy.36), calls=%async_computation.4 | async-start | bytes 262144 | tf_op jit(solution)/shard_map/all_to_all | solution.py:78
  139.7 6.5 %fusion.2 = f32[16,8,1536]{2,1,0:T(8,128)S(1)} fusion(bf16[16,8,4096]{2,1,0:T(8,128)(2,1)S(1)} %all-to-all-done.1, bf16[1,1,4096,1536]{3,2,1,0:T(8,128)(2,1)} %param.18), kind=kOutput, calls=%fused_computation.2 | convolution fusion | flops 1610612736 | bytes 14417920 | tf_op jit(solution)/shard_map/scd,df->scf/dot_general | solution.py:58
  147.4 1.6 copy.31
  149.0 6.0 %all-to-all-start.2 = ((bf16[16,8,4096]{2,1,0:T(8,128)(2,1)}), bf16[16,8,4096]{2,1,0:T(8,128)(2,1)S(1)}, u32[]{:S(2)}, u32[]{:S(2)}) async-start(bf16[16,8,4096]{2,1,0:T(8,128)(2,1)} %copy.31), calls=%async_computation.3 | async-start | bytes 2097152 | tf_op jit(solution)/shard_map/all_to_all | solution.py:66
  155.3 4.3 %fusion.16 = f32[128,4096]{1,0:T(8,128)} fusion(bf16[1,512,4096]{2,1,0:T(8,128)(2,1)} %param.16, bf16[8,16,512]{2,0,1:T(8,128)(2,1)S(1)} %all-to-all-done.3), kind=kOutput, calls=%fused_computation.16 | convolution fusion | flops 536870912 | bytes 6422528 | tf_op jit(solution)/shard_map/dot_general | solution.py:80
  160.5 17.4 %all-to-all-done.2 = bf16[16,8,4096]{2,1,0:T(8,128)(2,1)S(1)} async-done(((bf16[16,8,4096]{2,1,0:T(8,128)(2,1)}), bf16[16,8,4096]{2,1,0:T(8,128)(2,1)S(1)}, u32[]{:S(2)}, u32[]{:S(2)}) %all-to-all-start.2) | async-done | bytes 1048608 | tf_op jit(solution)/shard_map/all_to_all | solution.py:66
  180.8 42.1 %reduce-scatter.5.cloned.1.call-done = f32[8,4096]{1,0:T(8,128)} async-done(((f32[128,4096]{1,0:T(8,128)}), f32[8,4096]{1,0:T(8,128)}) %reduce-scatter.5.cloned.1.call-update) | async-done | bytes 131088 | tf_op jit(solution)/shard_map/reduce_scatter | solution.py:79
  225.4 28.7 %all_to_all.53 = bf16[16,8,4096]{2,1,0:T(8,128)(2,1)S(1)} all-to-all(bf16[16,8,4096]{2,1,0:T(8,128)(2,1)S(1)} %convolution_convert_fusion), channel_id=1, replica_groups=mesh['section'=2,'ep'=16] {'ep'}, dimensions={0} | all-to-all | bytes 2097152 | tf_op jit(solution)/shard_map/all_to_all | solution.py:104
  254.1 6.6 %fusion = f32[16,8,1536]{2,1,0:T(8,128)S(1)} fusion(bf16[16,8,4096]{2,1,0:T(8,128)(2,1)S(1)} %all_to_all.53, bf16[1,1,4096,1536]{3,2,1,0:T(8,128)(2,1)} %param.18), kind=kOutput, calls=%fused_computation | convolution fusion | flops 1610612736 | bytes 14417920 | tf_op jit(solution)/shard_map/scd,df->scf/dot_general | solution.py:58
  261.9 1.5 copy.40
  263.4 5.0 %all-to-all-start.5 = ((bf16[16,8,4096]{2,1,0:T(8,128)(2,1)}), bf16[16,8,4096]{2,1,0:T(8,128)(2,1)S(1)}, u32[]{:S(2)}, u32[]{:S(2)}) async-start(bf16[16,8,4096]{2,1,0:T(8,128)(2,1)} %copy.40), calls=%async_computation.7 | async-start | bytes 2097152 | tf_op jit(solution)/shard_map/all_to_all | solution.py:66
  268.5 22.9 %all-to-all-done.5 = bf16[16,8,4096]{2,1,0:T(8,128)(2,1)S(1)} async-done(((bf16[16,8,4096]{2,1,0:T(8,128)(2,1)}), bf16[16,8,4096]{2,1,0:T(8,128)(2,1)S(1)}, u32[]{:S(2)}, u32[]{:S(2)}) %all-to-all-start.5) | async-done | bytes 1048608 | tf_op jit(solution)/shard_map/all_to_all | solution.py:66
  (113 shorter events, 21.0 us)
Async XLA Ops:
  6.5 96.2 %reduce-scatter.3.cloned.1.call-start = ((), (), s32[]{:S(2)}) async-start(), calls=%async_computation.8 | async-start | bytes 2228224 | tf_op jit(solution)/shard_map/reduce_scatter | solution.py:79
  10.8 5.7 %copy-start.17 = (s32[2,8]{1,0:T(2,128)S(1)}, s32[2,8]{1,0:T(2,128)}, u32[]{:S(2)}) copy-start(s32[2,8]{1,0:T(2,128)} %param.15) | copy-start | bytes 196
  10.8 5.8 %copy-start.9 = (bf16[1,2,8,1024]{3,2,1,0:T(8,128)(2,1)S(1)}, bf16[1,2,8,1024]{3,2,1,0:T(8,128)(2,1)}, u32[]{:S(2)}) copy-start(bf16[1,2,8,1024]{3,2,1,0:T(8,128)(2,1)} %param.13) | copy-start | bytes 98308
  39.1 63.7 %copy-start.2 = (bf16[1,8,4096]{2,1,0:T(8,128)(2,1)S(1)}, bf16[1,8,4096]{2,1,0:T(8,128)(2,1)}, u32[]{:S(2)}) copy-start(bf16[1,8,4096]{2,1,0:T(8,128)(2,1)} %param.11) | copy-start | bytes 196612
  39.1 64.7 %copy-start.4 = (f32[1,4096]{1,0:T(1,128)S(1)}, f32[1,4096]{1,0:T(1,128)}, u32[]{:S(2)}) copy-start(f32[1,4096]{1,0:T(1,128)} %param.17) | copy-start | bytes 49156
  43.4 68.9 %copy-start.5 = (f32[8,512]{1,0:T(8,128)S(1)}, f32[8,512]{1,0:T(8,128)}, u32[]{:S(2)}) copy-start(f32[8,512]{1,0:T(8,128)} %get-tuple-element.24) | copy-start | bytes 49156
  43.4 68.9 %copy-start.15 = (bf16[8,4,128,1]{2,0,1,3:T(8,128)(2,1)S(1)}, bf16[8,4,128,1]{2,0,1,3:T(8,128)(2,1)}, u32[]{:S(2)}) copy-start(bf16[8,4,128,1]{2,0,1,3:T(8,128)(2,1)} %get-tuple-element.23) | copy-start | bytes 24580
  44.2 68.4 %copy-start.6 = (s32[1,1,8,8]{3,2,1,0:T(8,128)}, s32[1,1,8,8]{3,2,1,0:T(8,128)S(1)}, u32[]{:S(2)}) copy-start(s32[1,1,8,8]{3,2,1,0:T(8,128)S(1)} %copy.52) | copy-start | bytes 772
  44.7 67.9 %copy-start.10 = (s32[8,8]{1,0:T(8,128)}, s32[8,8]{1,0:T(8,128)S(1)}, u32[]{:S(2)}) copy-start(s32[8,8]{1,0:T(8,128)S(1)} %eq.117) | copy-start | bytes 772
  106.2 26.7 %all-to-all-start.1 = ((bf16[16,8,4096]{2,1,0:T(8,128)(2,1)}), bf16[16,8,4096]{2,1,0:T(8,128)(2,1)S(1)}, u32[]{:S(2)}, u32[]{:S(2)}) async-start(bf16[16,8,4096]{2,1,0:T(8,128)(2,1)} %convolution_convert_fusion.1), calls=%async_computation.2 | async-start | bytes 2097152 | tf_op jit(solution)/shard_map/all_to_all | solution.py:104
  115.8 30.6 %slice-start = ((s8[6291456]{0:T(1024)(128)(4,1)}), s8[2097152]{0:T(1024)(128)(4,1)S(1)}, s32[]{:S(2)}) async-start(s8[6291456]{0:T(1024)(128)(4,1)} %bitcast.140), calls=%async_computation.10 | async-start | bytes 4194304
  132.9 16.1 %all-to-all-start.3 = ((bf16[8,16,512]{2,0,1:T(8,128)(2,1)}), bf16[8,16,512]{2,0,1:T(8,128)(2,1)S(1)}, u32[]{:S(2)}, u32[]{:S(2)}) async-start(bf16[8,16,512]{2,0,1:T(8,128)(2,1)} %copy.36), calls=%async_computation.4 | async-start | bytes 262144 | tf_op jit(solution)/shard_map/all_to_all | solution.py:78
  139.7 6.7 %slice-start.1 = ((s8[6291456]{0:T(1024)(128)(4,1)}), s8[4194304]{0:T(1024)(128)(4,1)S(1)}, s32[]{:S(2)}) async-start(s8[6291456]{0:T(1024)(128)(4,1)} %bitcast.140), calls=%async_computation.11 | async-start | bytes 8388608
  149.0 29.0 %all-to-all-start.2 = ((bf16[16,8,4096]{2,1,0:T(8,128)(2,1)}), bf16[16,8,4096]{2,1,0:T(8,128)(2,1)S(1)}, u32[]{:S(2)}, u32[]{:S(2)}) async-start(bf16[16,8,4096]{2,1,0:T(8,128)(2,1)} %copy.31), calls=%async_computation.3 | async-start | bytes 2097152 | tf_op jit(solution)/shard_map/all_to_all | solution.py:66
  155.0 5.1 %copy-start.8 = (f32[1,2,8,8]{3,2,1,0:T(8,128)S(1)}, f32[1,2,8,8]{3,2,1,0:T(8,128)}, u32[]{:S(2)}) copy-start(f32[1,2,8,8]{3,2,1,0:T(8,128)} %param.21) | copy-start | bytes 1540
  155.0 5.4 %copy-start.11 = (s32[8,8]{1,0:T(8,128)S(1)}, s32[8,8]{1,0:T(8,128)}, u32[]{:S(2)}) copy-start(s32[8,8]{1,0:T(8,128)} %copy-done.10) | copy-start | bytes 772
  155.1 5.4 %copy-start.7 = (s32[1,1,8,8]{3,2,1,0:T(8,128)S(1)}, s32[1,1,8,8]{3,2,1,0:T(8,128)}, u32[]{:S(2)}) copy-start(s32[1,1,8,8]{3,2,1,0:T(8,128)} %copy-done.6) | copy-start | bytes 772
  155.1 67.9 %reduce-scatter.5.cloned.1.call-start = ((), (), s32[]{:S(2)}) async-start(), calls=%async_computation.9 | async-start | bytes 2228224 | tf_op jit(solution)/shard_map/reduce_scatter | solution.py:79
  159.5 19.4 %copy-start = (f32[8,4096]{1,0:T(8,128)S(1)}, f32[8,4096]{1,0:T(8,128)}, u32[]{:S(2)}) copy-start(f32[8,4096]{1,0:T(8,128)} %reduce-scatter.3.cloned.1.call-done) | copy-start | bytes 393220
  179.0 44.0 %collective-permute-start = (bf16[8,4096]{1,0:T(8,128)(2,1)S(1)}, bf16[8,4096]{1,0:T(8,128)(2,1)S(1)}, u32[]{:S(2)}, u32[]{:S(2)}) collective-permute-start(bf16[8,4096]{1,0:T(8,128)(2,1)S(1)} %add_convert_fusion.1), channel_id=1, source_target_pairs={{0,16},{16,0},{1,17},{17,1},{2,18},{18,2},{3,19},{19,3},{4,20},{20... | collective-permute-start | bytes 196616 | tf_op jit(solution)/shard_map/ppermute | solution.py:15
  225.4 35.4 %slice-start.2 = ((s8[6291456]{0:T(1024)(128)(4,1)}), s8[4194304]{0:T(1024)(128)(4,1)S(1)}, s32[]{:S(2)}) async-start(s8[6291456]{0:T(1024)(128)(4,1)} %bitcast.142), calls=%async_computation.12 | async-start | bytes 8388608
  254.1 6.7 %slice-start.3 = ((s8[6291456]{0:T(1024)(128)(4,1)}), s8[2097152]{0:T(1024)(128)(4,1)S(1)}, s32[]{:S(2)}) async-start(s8[6291456]{0:T(1024)(128)(4,1)} %bitcast.142), calls=%async_computation.13 | async-start | bytes 4194304
  261.9 30.5 %copy-start.1 = (f32[8,4096]{1,0:T(8,128)S(1)}, f32[8,4096]{1,0:T(8,128)}, u32[]{:S(2)}) copy-start(f32[8,4096]{1,0:T(8,128)} %reduce-scatter.5.cloned.1.call-done) | copy-start | bytes 393220
  263.4 27.9 %all-to-all-start.5 = ((bf16[16,8,4096]{2,1,0:T(8,128)(2,1)}), bf16[16,8,4096]{2,1,0:T(8,128)(2,1)S(1)}, u32[]{:S(2)}, u32[]{:S(2)}) async-start(bf16[16,8,4096]{2,1,0:T(8,128)(2,1)} %copy.40), calls=%async_computation.7 | async-start | bytes 2097152 | tf_op jit(solution)/shard_map/all_to_all | solution.py:66
  (5 other events, 17.2 us)
Sparse Core Ops, SparseCore 0:
  43.5 59.1 reduce-scatter.2
  160.1 62.8 reduce-scatter.4
where the time goes:
time: 302 us; the launch traced here: 300 us
  waiting for transfers between devices  156 us (52%)
  blocking collectives  43.8 us (15%)
  matrix products  33.9 us (11%)
  starting transfers between devices  23.4 us (8%)
  local copies, waits for them, and re-layouts  21.8 us (7%)
  between operations  13.9 us (5%)
  other arithmetic  6.7 us (2%)
    reduce_scatter x2, waiting for transfers between devices, layer_apply(): lax.psum_scatter(jnp.dot(head_rows, proj_rows, preferred_element_type=jnp...  99.8 us
    all_to_all x2, waiting for transfers between devices, send_back(): lax.all_to_all(results, 'ep', split_axis=0, concat_axis=0, tiled=True)  40.3 us
    all_to_all x1, blocking collectives, layer_apply(): lax.all_to_all(outgoing, 'ep', split_axis=0, concat_axis=0, tiled=True)  28.7 us
    all_to_all x1, waiting for transfers between devices, layer_apply(): lax.all_to_all(outgoing, 'ep', split_axis=0, concat_axis=0, tiled=True)  16.2 us
    all_to_all x1, blocking collectives, layer_apply(): lax.all_to_all(attn, 'ep', split_axis=1, concat_axis=0, tiled=True)  15.1 us
    dot_general x2, matrix products, expert_outputs(): jnp.einsum('scd,df->scf', slots, w_pair, preferred_element_type=jnp.float32)  13.1 us
    all_to_all x2, starting transfers between devices, send_back(): lax.all_to_all(results, 'ep', split_axis=0, concat_axis=0, tiled=True)  11 us
    dynamic_slice x3, local copies, waits for them, and re-layouts, on_device(): lax.dynamic_index_in_dim(kv_cache[0], micro, 0, keepdims=False)  10.5 us
  transfers between devices with their start and end apart: 7, of which 5 were waited for; matrix products, arithmetic and copies ran while one was open for 8% of the time, Pallas kernels for 0%

commit v1 on v0

v1 whole, which is shorter than its diff:
```python
import functools
import math

import jax
import jax.numpy as jnp
from jax import lax
from jax.experimental import pallas as pl
from jax.experimental.pallas import tpu as pltpu
from jax.sharding import PartitionSpec as P

HEADS = 64
KVH = 4
HD = 128
STEP_ROWS = 4
TILE = 512
UNIT_TILE = 256
MESH = pl.DeviceIdType.MESH


def attend_kernel(order_ref, len_ref, q_ref, new_ref, kv_ref, out_ref):
    group = HEADS // KVH
    scale = 1.0 / math.sqrt(HD)
    micro = order_ref[pl.program_id(0)]
    first = pl.program_id(1) * STEP_ROWS
    for row in range(STEP_ROWS):
        q = q_ref[0, row]
        newest = new_ref[0, row].astype(jnp.float32)
        span = len_ref[micro, first + row]
        scores = (
            jnp.concatenate(
                [
                    lax.dot_general(
                        q[g * group : (g + 1) * group],
                        kv_ref[0, row, :, g * HD : (g + 1) * HD],
                        (((1,), (1,)), ((), ())),
                        preferred_element_type=jnp.float32,
                    )
                    for g in range(KVH)
                ],
                axis=0,
            )
            * scale
        )
        new_keys = jnp.concatenate(
            [jnp.broadcast_to(newest[g : g + 1], (group, HD)) for g in range(KVH)], axis=0
        )
        new_values = jnp.concatenate(
            [jnp.broadcast_to(newest[KVH + g : KVH + g + 1], (group, HD)) for g in range(KVH)],
            axis=0,
        )
        fresh = jnp.sum(q.astype(jnp.float32) * new_keys, axis=-1, keepdims=True) * scale
        valid = lax.broadcasted_iota(jnp.int32, scores.shape, 1) < span
        top = jnp.maximum(
            jnp.max(jnp.where(valid, scores, -jnp.inf), axis=-1, keepdims=True), fresh
        )
        expo = jnp.where(valid, jnp.exp(scores - top), 0.0)
        expo_new = jnp.exp(fresh - top)
        total = jnp.sum(expo, axis=-1, keepdims=True) + expo_new
        probs = (expo / total).astype(jnp.bfloat16)
        probs_new = (expo_new / total).astype(jnp.bfloat16).astype(jnp.float32)
        mixed = jnp.concatenate(
            [
                jnp.dot(
                    probs[g * group : (g + 1) * group],
                    kv_ref[0, row, :, (KVH + g) * HD : (KVH + g + 1) * HD],
                    preferred_element_type=jnp.float32,
                )
                for g in range(KVH)
            ],
            axis=0,
        )
        out_ref[0, row] = (mixed + probs_new * new_values).astype(jnp.bfloat16)


def attend_all(order, lengths, query, newest, cache):
    micros, rows = query.shape[:2]
    positions = cache.shape[2]
    q = query.reshape(micros, rows, HEADS, HD)
    new = newest.reshape(micros, rows, 2 * KVH, HD)

    def taken(*rest):
        return lambda t, i, order, spans: (order[t], i) + rest

    return pl.pallas_call(
        attend_kernel,
        out_shape=jax.ShapeDtypeStruct((micros, rows, HEADS, HD), jnp.bfloat16),
        grid_spec=pltpu.PrefetchScalarGridSpec(
            num_scalar_prefetch=2,
            grid=(micros, rows // STEP_ROWS),
            in_specs=[
                pl.BlockSpec((1, STEP_ROWS, HEADS, HD), taken(0, 0)),
                pl.BlockSpec((1, STEP_ROWS, 2 * KVH, HD), taken(0, 0)),
                pl.BlockSpec((1, STEP_ROWS, positions, 2 * KVH * HD), taken(0, 0)),
            ],
            out_specs=pl.BlockSpec(
                (1, STEP_ROWS, HEADS, HD), lambda t, i, order, spans: (t, i, 0, 0)
            ),
        ),
        compiler_params=pltpu.CompilerParams(vmem_limit_bytes=16 << 20),
    )(order, lengths, q, new, cache)


def folded(rows):
    half = rows.shape[1] // 2
    return jnp.concatenate([rows[:, :half], rows[:, half:]], axis=0).astype(jnp.bfloat16)


def unfolded(block):
    wide = block.astype(jnp.float32)
    half = wide.shape[0] // 2
    return jnp.concatenate([wide[:half], wide[half:]], axis=1)


def layers_kernel(n, sections, a_ref, share_ref, hidden_ref, gain_ref, wo_hbm, wgu_hbm, wd_hbm, out_ref, *scratch):
    levels = n.bit_length() - 1
    (wo, wgu, wd, a_all, share_all, x_all, units, x_out, x_in, h_out, h_in) = scratch[:11]
    rest = scratch[11:]
    acc = rest[:2]
    sent = (rest[2 : 2 + levels], rest[2 + levels : 2 + 2 * levels])
    got = (rest[2 + 2 * levels : 2 + 3 * levels], rest[2 + 3 * levels : 2 + 4 * levels])
    (w_sem, own_sem, a_send, a_recv, s_send, s_recv, r_send, r_recv, g_send, g_recv, h_send, h_recv) = rest[2 + 4 * levels :]

    me = lax.axis_index("ep")
    stage = lax.axis_index("section")
    rows = hidden_ref.shape[0]
    width = hidden_ref.shape[1]
    cols = a_all.shape[2]
    bits = [(me // (1 << j)) % 2 for j in range(levels)]

    def flipped(j):
        return me + (1 - 2 * bits[j]) * (1 << j)

    place = sum(bits[j] * (1 << (levels - 1 - j)) for j in range(levels))

    loads = [
        pltpu.make_async_copy(src, dst, w_sem.at[i])
        for i, (src, dst) in enumerate(((wo_hbm, wo), (wgu_hbm, wgu), (wd_hbm, wd)))
    ]
    for load in loads:
        load.start()

    barrier = pltpu.get_barrier_semaphore()

    @pl.loop(1, n)
    def _(d):
        pl.semaphore_signal(
            barrier, inc=1, device_id={"ep": lax.rem(me + d, n)}, device_id_type=MESH
        )

    for d in range(1, sections):
        pl.semaphore_signal(
            barrier,
            inc=1,
            device_id={"section": lax.rem(stage + d, sections)},
            device_id_type=MESH,
        )
    pl.semaphore_wait(barrier, n - 1 + sections - 1)

    def a_part(peer):
        return a_ref.at[:, pl.ds(pl.multiple_of(peer * cols, cols), cols)]

    def exchange(d):
        peer = lax.rem(me + d, n)
        return (
            pltpu.make_async_remote_copy(
                src_ref=a_part(peer),
                dst_ref=a_all.at[place],
                send_sem=a_send.at[d],
                recv_sem=a_recv.at[d],
                device_id={"ep": peer},
                device_id_type=MESH,
            ),
            pltpu.make_async_remote_copy(
                src_ref=share_ref.at[peer],
                dst_ref=share_all.at[place],
                send_sem=s_send.at[d],
                recv_sem=s_recv.at[d],
                device_id={"ep": peer},
                device_id_type=MESH,
            ),
        )

    @pl.loop(1, n)
    def _(d):
        for copy in exchange(d):
            copy.start()

    own = (
        pltpu.make_async_copy(a_part(me), a_all.at[place], own_sem.at[0]),
        pltpu.make_async_copy(share_ref.at[me], share_all.at[place], own_sem.at[1]),
    )
    for copy in own:
        copy.start()
    for copy in own:
        copy.wait()

    @pl.loop(1, n)
    def _(d):
        for copy in exchange(d):
            copy.wait()

    core = bits[0] == 1
    half = n * rows // 2

    def keep_and_send(c, partial, at):
        low, high = partial[:half], partial[half:]
        acc[c][:, at] = jnp.where(core, high, low)
        sent[c][0][:, at] = jnp.where(core, low, high).astype(jnp.bfloat16)

    def reduce_copy(c, call, j):
        return pltpu.make_async_remote_copy(
            src_ref=sent[c][j],
            dst_ref=got[c][j],
            send_sem=r_send.at[call, j],
            recv_sem=r_recv.at[call, j],
            device_id={"ep": flipped(j)},
            device_id_type=MESH,
        )

    def advance(c, call, j):
        reduce_copy(c, call, j - 1).wait()
        size = half >> j
        if j < levels - 1:
            keep = pl.ds(pl.multiple_of(bits[j] * size, size), size)
            send = pl.ds(pl.multiple_of((1 - bits[j]) * size, size), size)
            sent[c][j][...] = (
                acc[c][send, :] + got[c][j - 1][send, :].astype(jnp.float32)
            ).astype(jnp.bfloat16)
            reduce_copy(c, call, j).start()
            acc[c][:size, :] = acc[c][keep, :] + got[c][j - 1][keep, :].astype(jnp.float32)
        else:
            both = acc[c][: 2 * size, :] + got[c][j - 1][...].astype(jnp.float32)
            upper = bits[j] == 1
            low, high = both[:size], both[size:]
            sent[c][j][...] = folded(jnp.where(upper, low, high))
            reduce_copy(c, call, j).start()
            acc[c][:size, :] = jnp.where(upper, high, low)

    def total(c, call):
        reduce_copy(c, call, levels - 1).wait()
        return acc[c][:rows, :] + unfolded(got[c][levels - 1][...])

    def gather(tick, x):
        x_out[...] = folded(x)
        copy = pltpu.make_async_remote_copy(
            src_ref=x_out,
            dst_ref=x_in,
            send_sem=g_send.at[tick, levels - 1],
            recv_sem=g_recv.at[tick, levels - 1],
            device_id={"ep": flipped(levels - 1)},
            device_id_type=MESH,
        )
        copy.start()
        copy.wait()
        other = unfolded(x_in[...])
        upper = bits[levels - 1] == 1
        pair = jnp.concatenate([jnp.where(upper, other, x), jnp.where(upper, x, other)], axis=0)
        pair_at = pl.multiple_of((place // 2) * (2 * rows), 2 * rows)
        x_all[pl.ds(pair_at, 2 * rows), :] = pair.astype(jnp.bfloat16)
        for j in range(levels - 2, -1, -1):
            blocks = 1 << (levels - 1 - j)
            size = rows * blocks
            held = x_all.at[pl.ds(pl.multiple_of((place // blocks) * size, size), size)]
            copy = pltpu.make_async_remote_copy(
                src_ref=held,
                dst_ref=held,
                send_sem=g_send.at[tick, j],
                recv_sem=g_recv.at[tick, j],
                device_id={"ep": flipped(j)},
                device_id_type=MESH,
            )
            copy.start()
            copy.wait()

    loads[0].wait()

    @pl.loop(0, width // TILE)
    def _(i):
        at = pl.ds(pl.multiple_of(i * TILE, TILE), TILE)
        product = jnp.dot(
            a_all[...].reshape(n * 2 * rows, cols), wo[:, at], preferred_element_type=jnp.float32
        ).reshape(n, 2 * rows, TILE)
        keep_and_send(0, product[:, :rows].reshape(n * rows, TILE), at)
        keep_and_send(1, product[:, rows:].reshape(n * rows, TILE), at)

    reduce_copy(0, 0, 0).start()
    reduce_copy(1, 1, 0).start()
    for j in range(1, levels):
        advance(0, 0, j)

    hidden = hidden_ref[...].astype(jnp.float32)
    later = list(range(1, levels))
    for tick in range(2):
        h_att = hidden + total(tick, tick)
        meansq = jnp.mean(h_att * h_att, axis=-1, keepdims=True)
        x = h_att * lax.rsqrt(meansq + 1e-06) * gain_ref[...]
        gather(tick, x)
        if tick == 0:
            loads[1].wait()
            if later:
                advance(1, 1, later.pop(0))
        units_wide = units.shape[1]

        @pl.loop(0, units_wide // UNIT_TILE)
        def _(i):
            at = pl.multiple_of(i * UNIT_TILE, UNIT_TILE)
            gate = jnp.dot(
                x_all[...], wgu[:, pl.ds(at, UNIT_TILE)], preferred_element_type=jnp.float32
            )
            up_at = pl.multiple_of(units_wide + i * UNIT_TILE, UNIT_TILE)
            up = jnp.dot(
                x_all[...], wgu[:, pl.ds(up_at, UNIT_TILE)], preferred_element_type=jnp.float32
            )
            units[:, pl.ds(at, UNIT_TILE)] = (gate / (1.0 + jnp.exp(-gate)) * up).astype(
                jnp.bfloat16
            )

        if tick == 0:
            loads[2].wait()
            if later:
                advance(1, 1, later.pop(0))

        share = share_all[:, tick * rows : (tick + 1) * rows, :].reshape(n * rows, 128)[:, :1]

        @pl.loop(0, width // TILE)
        def _(i):
            at = pl.ds(pl.multiple_of(i * TILE, TILE), TILE)
            keep_and_send(
                0, jnp.dot(units[...], wd[:, at], preferred_element_type=jnp.float32) * share, at
            )

        call = 2 + tick
        reduce_copy(0, call, 0).start()
        if tick == 0:
            while later:
                advance(1, 1, later.pop(0))
        for j in range(1, levels):
            advance(0, call, j)
        done = h_att + total(0, call)
        if tick == 0:
            h_out[...] = folded(done)
            copy = pltpu.make_async_remote_copy(
                src_ref=h_out,
                dst_ref=h_in,
                send_sem=h_send,
                recv_sem=h_recv,
                device_id={"section": lax.rem(stage + 1, sections)},
                device_id_type=MESH,
            )
            copy.start()
            copy.wait()
            hidden = unfolded(h_in[...])
        else:
            out_ref[...] = done.astype(jnp.bfloat16)


def layers_all(n, sections, attn, share, hidden, gain, proj_rows, w_pair, w_out):
    levels = n.bit_length() - 1
    rows, width = hidden.shape
    cols = proj_rows.shape[0]
    vmem, dma = pltpu.VMEM, pltpu.SemaphoreType.DMA
    bf16, f32 = jnp.bfloat16, jnp.float32
    folded_shape = (2 * rows, width // 2)
    halves = [vmem((n * rows >> (j + 1), width), bf16) for j in range(levels - 1)]
    halves.append(vmem(folded_shape, bf16))
    return pl.pallas_call(
        functools.partial(layers_kernel, n, sections),
        out_shape=jax.ShapeDtypeStruct((rows, width), bf16),
        in_specs=[pl.BlockSpec(memory_space=pltpu.VMEM)] * 4
        + [pl.BlockSpec(memory_space=pl.ANY)] * 3,
        out_specs=pl.BlockSpec(memory_space=pltpu.VMEM),
        scratch_shapes=[
            vmem(proj_rows.shape, bf16),
            vmem(w_pair.shape, bf16),
            vmem(w_out.shape, bf16),
            vmem((n, 2 * rows, cols), bf16),
            vmem((n, 2 * rows, 128), f32),
            vmem((n * rows, width), bf16),
            vmem((n * rows, w_out.shape[0]), bf16),
            vmem(folded_shape, bf16),
            vmem(folded_shape, bf16),
            vmem(folded_shape, bf16),
            vmem(folded_shape, bf16),
        ]
        + [vmem((n * rows // 2, width), f32)] * 2
        + halves * 4
        + [
            dma((3,)),
            dma((2,)),
            dma((n,)),
            dma((n,)),
            dma((n,)),
            dma((n,)),
            dma((4, levels)),
            dma((4, levels)),
            dma((2, levels)),
            dma((2, levels)),
            dma(()),
            dma(()),
        ],
        compiler_params=pltpu.CompilerParams(
            collective_id=0, has_side_effects=True, vmem_limit_bytes=60 << 20
        ),
        cost_estimate=pl.CostEstimate(
            flops=int(2 * n * rows * width * (2 * cols + 6 * w_out.shape[0])),
            bytes_accessed=int(2 * width * (cols + 3 * w_out.shape[0])),
            transcendentals=0,
        ),
    )(attn, share, hidden, gain, proj_rows, w_pair, w_out)


def on_device(
    n,
    sections,
    hidden_in,
    query,
    new_kv,
    kv_cache,
    lengths,
    out_proj,
    norm_gain,
    w_gate_up,
    w_down,
    expert_ids,
    route_weight,
):
    position = lax.axis_index("section")
    member = lax.axis_index("ep")
    rows = hidden_in.shape[1]
    order = (position - jnp.arange(2, dtype=jnp.int32)) % 2
    attn = attend_all(order, lengths, query[0], new_kv[0], kv_cache[0])
    picks = lax.dynamic_slice_in_dim(expert_ids[0], member * rows, rows, 1)
    weights = route_weight[0]
    share = weights / jnp.sum(weights, axis=-1, keepdims=True)
    swap = position == 1
    picks = jnp.where(swap, picks[::-1], picks).reshape(2 * rows, -1)
    share = jnp.where(swap, share[::-1], share).reshape(2 * rows, -1)
    chosen = picks[None] == jnp.arange(n, dtype=jnp.int32)[:, None, None]
    dense = jnp.sum(jnp.where(chosen, share[None], 0.0), axis=-1)
    return layers_all(
        n,
        sections,
        attn.reshape(2 * rows, HEADS * HD),
        jnp.broadcast_to(dense[:, :, None], (n, 2 * rows, 128)),
        hidden_in[0],
        norm_gain,
        out_proj[0],
        w_gate_up[0, 0],
        w_down[0, 0],
    )[None]


def solution(mesh):
    in_specs = (
        P("section", "ep", None),
        P("section", None, "ep", None),
        P("section", None, "ep", None),
        P("section", None, "ep", None, None),
        P(None, "ep"),
        P("section", "ep", None),
        P("section", None),
        P("section", "ep", None, None),
        P("section", "ep", None, None),
        P("section", None, None, None),
        P("section", None, "ep", None),
    )
    out_specs = P("section", "ep", None)
    return jax.shard_map(
        functools.partial(on_device, mesh.shape["ep"], mesh.shape["section"]),
        mesh=mesh,
        in_specs=in_specs,
        out_specs=out_specs,
        check_vma=False,
    )
```

time: 302 us -> 142 us (0.47)
  waiting for transfers between devices: 156 us -> 0 us
  Pallas kernels: 0 us -> 131 us
  blocking collectives: 43.8 us -> 0 us
  matrix products: 33.9 us -> 0 us
  starting transfers between devices: 23.4 us -> 0 us
  between operations: 13.9 us -> 0.03 us
  local copies, waits for them, and re-layouts: 21.8 us -> 8.03 us
  other arithmetic: 6.7 us -> 1.61 us
    pallas_call x0 -> x2, Pallas kernels: none -> 131 us  [the longest x1 125 us: layers_all(): pl.pallas_call(functools.partial(layers_kernel, n, sections), out_shape=j...]
    reduce_scatter x2 -> x0, waiting for transfers between devices: 99.8 us -> none  [layer_apply(): lax.psum_scatter(jnp.dot(head_rows, proj_rows, preferred_element_type=jnp...]
    all_to_all x4 -> x0, waiting for transfers between devices: 56.5 us -> none  [the longest x2 40.3 us: send_back(): lax.all_to_all(results, 'ep', split_axis=0, concat_axis=0, tiled=True)]
    all_to_all x2 -> x0, blocking collectives: 43.8 us -> none  [the longest x1 28.7 us: layer_apply(): lax.all_to_all(outgoing, 'ep', split_axis=0, concat_axis=0, tiled=True)]
    dot_general x18 -> x0, matrix products: 33.9 us -> none  [the longest x2 13.1 us: expert_outputs(): jnp.einsum('scd,df->scf', slots, w_pair, preferred_element_type=jnp.float32)]
    all_to_all x4 -> x0, starting transfers between devices: 21.6 us -> none  [the longest x2 11 us: send_back(): lax.all_to_all(results, 'ep', split_axis=0, concat_axis=0, tiled=True)]
    dynamic_slice x4 -> x1, local copies, waits for them, and re-layouts: 11.2 us -> 0.07 us  [on_device(): picks = lax.dynamic_slice_in_dim(expert_ids[0], member * rows, rows, 1)]
    unnamed x49 -> x11, local copies, waits for them, and re-layouts: 0.3 us -> 7.05 us
  transfers between devices with their start and end apart: 7 -> 0, of which waited for: 5 -> 0; matrix products, arithmetic and copies ran while one was open for 8% -> 0% of each run, Pallas kernels for 0% -> 0%
where the time goes in v1:
time: 142 us; the launch traced here: 141 us
  Pallas kernels  131 us (92%)
  local copies, waits for them, and re-layouts  8.03 us (6%)
  other arithmetic  1.61 us (1%)
    pallas_call x1, Pallas kernels, layers_all(): pl.pallas_call(functools.partial(layers_kernel, n, sections), out_shape=j...  125 us
    unnamed x11, local copies, waits for them, and re-layouts  7.05 us
    pallas_call x1, Pallas kernels, attend_all(): pl.pallas_call(attend_kernel, out_shape=jax.ShapeDtypeStruct((micros, row...  6.67 us

profile of v1, /device:TPU:0, one launch (start us, length us, event | category | flops | bytes accessed | tf_op | source)
XLA Modules:
  0.0 141.1 jit_solution(7861868760055749020)
XLA Ops:
  0.0 0.0 copy-start
  0.0 1.0 copy.30
  1.0 0.8 copy.31
  1.8 0.0 copy-start.1
  1.8 2.2 %copy-done.1 = bf16[1,2,8,128,1024]{4,3,2,1,0:T(8,128)(2,1)S(1)} copy-done((bf16[1,2,8,128,1024]{4,3,2,1,0:T(8,128)(2,1)S(1)}, bf16[1,2,8,128,1024]{4,3,2,1,0:T(8,128)(2,1)}, u32[]{:S(2)}) %copy-start.1) | copy-done | bytes 4194328
  4.0 0.0 copy-start.2
  4.0 0.7 copy-done.2
  4.7 6.7 %shard_map.109 = bf16[2,8,64,128]{3,2,1,0:T(8,128)(2,1)S(1)} custom-call(s32[2]{0:T(128)S(1)} %and_select_fusion.order_ref, s32[2,8]{1,0:T(2,128)S(1)} %copy-done.2, bf16[2,8,64,128]{3,2,1,0:T(8,128)(2,1)S(1)} %copy.30, bf16[2,8,8,128]{3,2,1,0:T(8,128)(2,1)S(1)} %copy.31, bf16[2,8,128,1024]{3,2,1,0:T(8,128)(2,1)S(1)} %bitcast.32), custom_call_target="tpu_custom_call" | custom-call | tf_op jit(solution)/shard_map/pallas_call | solution.py:84
  11.3 0.9 copy.29
  12.2 0.8 reduce_sum.18
  13.0 0.8 bitcast_divide_fusion
  13.8 0.1 copy.21
  13.8 0.0 copy-done
  13.8 0.1 constant_dynamic-slice_fusion
  13.9 0.1 copy.22
  14.0 0.1 copy.20
  14.1 0.8 broadcast_in_dim.28.share_ref
  14.9 124.8 %shard_map.110 = bf16[8,4096]{1,0:T(8,128)(2,1)} custom-call(bf16[16,8192]{1,0:T(8,128)(2,1)} %bitcast.36, f32[16,16,128]{2,1,0:T(8,128)} %broadcast_in_dim.28.share_ref, bf16[8,4096]{1,0:T(8,128)(2,1)} %bitcast.39, f32[1,4096]{1,0:T(1,128)} %gain_ref.1, bf16[512,4096]{1,0:T(8,128)(2,1)} %bitcast.35, bf16[4096,1536]{1,0:T(8,128)(2,1)} %bitcast.33, ...), custom_call_target="tpu_custom_call" | custom-call | flops 5905580032 | bytes 23068672 | tf_op jit(solution)/shard_map/pallas_call | solution.py:366
  139.6 1.5 %copy.33 = bf16[1,8,4096]{2,1,0:T(8,128)(2,1)} copy(bf16[1,8,4096]{2,1,0:T(8,128)(2,1)} %bitcast.37) | data formatting | bytes 131072
  (4 shorter events, 0.1 us)
Async XLA Ops:
  0.0 13.8 %copy-start = (s32[1,2,128,8]{2,3,1,0:T(8,128)S(1)}, s32[1,2,128,8]{2,3,1,0:T(8,128)}, u32[]{:S(2)}) copy-start(s32[1,2,128,8]{2,3,1,0:T(8,128)} %param.20) | copy-start | bytes 24580
  1.8 2.2 %copy-start.1 = (bf16[1,2,8,128,1024]{4,3,2,1,0:T(8,128)(2,1)S(1)}, bf16[1,2,8,128,1024]{4,3,2,1,0:T(8,128)(2,1)}, u32[]{:S(2)}) copy-start(bf16[1,2,8,128,1024]{4,3,2,1,0:T(8,128)(2,1)} %param.14) | copy-start | bytes 12582916
  4.0 0.7 copy-start.2

commit v2 on v1

--- a/solution.py
+++ b/solution.py
@@ -113,31 +113,48 @@
 
 def layers_kernel(n, sections, a_ref, share_ref, hidden_ref, gain_ref, wo_hbm, wgu_hbm, wd_hbm, out_ref, *scratch):
     levels = n.bit_length() - 1
-    (wo, wgu, wd, a_all, share_all, x_all, units, x_out, x_in, h_out, h_in) = scratch[:11]
-    rest = scratch[11:]
-    acc = rest[:2]
-    sent = (rest[2 : 2 + levels], rest[2 + levels : 2 + 2 * levels])
-    got = (rest[2 + 2 * levels : 2 + 3 * levels], rest[2 + 3 * levels : 2 + 4 * levels])
-    (w_sem, own_sem, a_send, a_recv, s_send, s_recv, r_send, r_recv, g_send, g_recv, h_send, h_recv) = rest[2 + 4 * levels :]
+    (wo, wgu, wd, a_all, share_all, units, h_out, h_in) = scratch[:8]
+    x_all, x_out, x_in = scratch[8:10], scratch[10:12], scratch[12:14]
+    rest = scratch[14:]
+    acc = (rest[:2], rest[2:4])
+    rest = rest[4:]
+    parts = [rest[i * levels : (i + 1) * levels] for i in range(8)]
+    sent = (parts[0:2], parts[2:4])
+    got = (parts[4:6], parts[6:8])
+    (w_sem, own_sem, a_send, a_recv, s_send, s_recv, r_send, r_recv, g_send, g_recv, h_send, h_recv) = rest[8 * levels :]
 
     me = lax.axis_index("ep")
     stage = lax.axis_index("section")
     rows = hidden_ref.shape[0]
     width = hidden_ref.shape[1]
+    span = width // 2
     cols = a_all.shape[2]
     bits = [(me // (1 << j)) % 2 for j in range(levels)]
+    orders = (list(range(levels)), [0] + list(range(2, levels)) + [1])
+    places = [
+        sum(bits[order[i]] * (1 << (levels - 1 - i)) for i in range(levels)) for order in orders
+    ]
+    place = places[0]
+
+    def first_place(second):
+        owner = sum(
+            ((second >> (levels - 1 - i)) & 1) << orders[1][i] for i in range(levels)
+        )
+        return sum(((owner >> i) & 1) << (levels - 1 - i) for i in range(levels))
+
+    to_first = [first_place(second) for second in range(n)]
+
+    def reordered(value, blocks):
+        return jnp.concatenate([value[b * rows : (b + 1) * rows] for b in blocks], axis=0)
 
     def flipped(j):
         return me + (1 - 2 * bits[j]) * (1 << j)
-
-    place = sum(bits[j] * (1 << (levels - 1 - j)) for j in range(levels))
 
     loads = [
         pltpu.make_async_copy(src, dst, w_sem.at[i])
         for i, (src, dst) in enumerate(((wo_hbm, wo), (wgu_hbm, wgu), (wd_hbm, wd)))
     ]
-    for load in loads:
-        load.start()
+    loads[0].start()
 
     barrier = pltpu.get_barrier_semaphore()
 
@@ -180,10 +197,11 @@
             ),
         )
 
-    @pl.loop(1, n)
-    def _(d):
-        for copy in exchange(d):
-            copy.start()
+    for which in range(2):
+
+        @pl.loop(1, n)
+        def _(d):
+            exchange(d)[which].start()
 
     own = (
         pltpu.make_async_copy(a_part(me), a_all.at[place], own_sem.at[0]),
@@ -196,97 +214,120 @@
 
     @pl.loop(1, n)
     def _(d):
-        for copy in exchange(d):
-            copy.wait()
+        exchange(d)[0].wait()
 
     core = bits[0] == 1
     half = n * rows // 2
 
-    def keep_and_send(c, partial, at):
+    def keep_and_send(c, h, partial, at):
+        if h == 1:
+            partial = reordered(partial, to_first)
         low, high = partial[:half], partial[half:]
-        acc[c][:, at] = jnp.where(core, high, low)
-        sent[c][0][:, at] = jnp.where(core, low, high).astype(jnp.bfloat16)
-
-    def reduce_copy(c, call, j):
+        acc[c][h][:, at] = jnp.where(core, high, low)
+        sent[c][h][0][:, at] = jnp.where(core, low, high).astype(jnp.bfloat16)
+
+    def reduce_copy(c, call, h, j):
         return pltpu.make_async_remote_copy(
-            src_ref=sent[c][j],
-            dst_ref=got[c][j],
-            send_sem=r_send.at[call, j],
-            recv_sem=r_recv.at[call, j],
-            device_id={"ep": flipped(j)},
+            src_ref=sent[c][h][j],
+            dst_ref=got[c][h][j],
+            send_sem=r_send.at[2 * call + h, j],
+            recv_sem=r_recv.at[2 * call + h, j],
+            device_id={"ep": flipped(orders[h][j])},
             device_id_type=MESH,
         )
 
     def advance(c, call, j):
-        reduce_copy(c, call, j - 1).wait()
         size = half >> j
-        if j < levels - 1:
-            keep = pl.ds(pl.multiple_of(bits[j] * size, size), size)
-            send = pl.ds(pl.multiple_of((1 - bits[j]) * size, size), size)
-            sent[c][j][...] = (
-                acc[c][send, :] + got[c][j - 1][send, :].astype(jnp.float32)
-            ).astype(jnp.bfloat16)
-            reduce_copy(c, call, j).start()
-            acc[c][:size, :] = acc[c][keep, :] + got[c][j - 1][keep, :].astype(jnp.float32)
+        for h in range(2):
+            mine = bits[orders[h][j]]
+            sums, before = acc[c][h], got[c][h][j - 1]
+            reduce_copy(c, call, h, j - 1).wait()
+            if j < levels - 1:
+                keep = pl.ds(pl.multiple_of(mine * size, size), size)
+                send = pl.ds(pl.multiple_of((1 - mine) * size, size), size)
+                sent[c][h][j][...] = (
+                    sums[send, :] + before[send, :].astype(jnp.float32)
+                ).astype(jnp.bfloat16)
+                reduce_copy(c, call, h, j).start()
+                sums[:size, :] = sums[keep, :] + before[keep, :].astype(jnp.float32)
+            else:
+                both = sums[: 2 * size, :] + before[...].astype(jnp.float32)
+                upper = mine == 1
+                low, high = both[:size], both[size:]
+                sent[c][h][j][...] = folded(jnp.where(upper, low, high))
+                reduce_copy(c, call, h, j).start()
+                sums[:size, :] = jnp.where(upper, high, low)
+
+    def total(c, call):
+        sums = []
+        for h in range(2):
+            reduce_copy(c, call, h, levels - 1).wait()
+            sums.append(acc[c][h][:rows, :] + unfolded(got[c][h][levels - 1][...]))
+        return jnp.concatenate(sums, axis=1)
+
+    def gather_copy(tick, h, i):
+        if i == levels - 1:
+            src, dst = x_out[h], x_in[h]
         else:
-            both = acc[c][: 2 * size, :] + got[c][j - 1][...].astype(jnp.float32)
-            upper = bits[j] == 1
-            low, high = both[:size], both[size:]
-            sent[c][j][...] = folded(jnp.where(upper, low, high))
-            reduce_copy(c, call, j).start()
-            acc[c][:size, :] = jnp.where(upper, high, low)
-
-    def total(c, call):
-        reduce_copy(c, call, levels - 1).wait()
-        return acc[c][:rows, :] + unfolded(got[c][levels - 1][...])
+            blocks = 1 << (levels - 1 - i)
+            size = rows * blocks
+            at = pl.ds(pl.multiple_of((places[h] // blocks) * size, size), size)
+            src = dst = x_all[h].at[at]
+        return pltpu.make_async_remote_copy(
+            src_ref=src,
+            dst_ref=dst,
+            send_sem=g_send.at[2 * tick + h, i],
+            recv_sem=g_recv.at[2 * tick + h, i],
+            device_id={"ep": flipped(orders[h][i])},
+            device_id_type=MESH,
+        )
 
     def gather(tick, x):
-        x_out[...] = folded(x)
-        copy = pltpu.make_async_remote_copy(
-            src_ref=x_out,
-            dst_ref=x_in,
-            send_sem=g_send.at[tick, levels - 1],
-            recv_sem=g_recv.at[tick, levels - 1],
-            device_id={"ep": flipped(levels - 1)},
-            device_id_type=MESH,
-        )
-        copy.start()
-        copy.wait()
-        other = unfolded(x_in[...])
-        upper = bits[levels - 1] == 1
-        pair = jnp.concatenate([jnp.where(upper, other, x), jnp.where(upper, x, other)], axis=0)
-        pair_at = pl.multiple_of((place // 2) * (2 * rows), 2 * rows)
-        x_all[pl.ds(pair_at, 2 * rows), :] = pair.astype(jnp.bfloat16)
-        for j in range(levels - 2, -1, -1):
-            blocks = 1 << (levels - 1 - j)
-            size = rows * blocks
-            held = x_all.at[pl.ds(pl.multiple_of((place // blocks) * size, size), size)]
-            copy = pltpu.make_async_remote_copy(
-                src_ref=held,
-                dst_ref=held,
-                send_sem=g_send.at[tick, j],
-                recv_sem=g_recv.at[tick, j],
-                device_id={"ep": flipped(j)},
-                device_id_type=MESH,
-            )
-            copy.start()
-            copy.wait()
+        for h in range(2):
+            x_out[h][...] = folded(x[:, h * span : (h + 1) * span])
+            gather_copy(tick, h, levels - 1).start()
+        for i in range(levels - 2, -2, -1):
+            for h in range(2):
+                gather_copy(tick, h, i + 1).wait()
+                if i == levels - 2:
+                    own_x = x[:, h * span : (h + 1) * span]
+                    other = unfolded(x_in[h][...])
+                    upper = bits[orders[h][levels - 1]] == 1
+                    pair = jnp.concatenate(
+                        [jnp.where(upper, other, own_x), jnp.where(upper, own_x, other)], axis=0
+                    )
+                    pair_at = pl.multiple_of((places[h] // 2) * (2 * rows), 2 * rows)
+                    x_all[h][pl.ds(pair_at, 2 * rows), :] = pair.astype(jnp.bfloat16)
+                if i >= 0:
+                    gather_copy(tick, h, i).start()
 
     loads[0].wait()
-
-    @pl.loop(0, width // TILE)
-    def _(i):
-        at = pl.ds(pl.multiple_of(i * TILE, TILE), TILE)
-        product = jnp.dot(
-            a_all[...].reshape(n * 2 * rows, cols), wo[:, at], preferred_element_type=jnp.float32
-        ).reshape(n, 2 * rows, TILE)
-        keep_and_send(0, product[:, :rows].reshape(n * rows, TILE), at)
-        keep_and_send(1, product[:, rows:].reshape(n * rows, TILE), at)
-
-    reduce_copy(0, 0, 0).start()
-    reduce_copy(1, 1, 0).start()
+    loads[1].start()
+    loads[2].start()
+    for h in range(2):
+
+        @pl.loop(0, span // TILE)
+        def _(i):
+            at = pl.ds(pl.multiple_of(i * TILE, TILE), TILE)
+            product = jnp.dot(
+                a_all[...].reshape(n * 2 * rows, cols),
+                wo[:, pl.ds(pl.multiple_of(h * span + i * TILE, TILE), TILE)],
+                preferred_element_type=jnp.float32,
+            ).reshape(n, 2 * rows, TILE)
+            keep_and_send(0, h, product[:, :rows].reshape(n * rows, TILE), at)
+            keep_and_send(1, h, product[:, rows:].reshape(n * rows, TILE), at)
+
+        reduce_copy(0, 0, h, 0).start()
+
     for j in range(1, levels):
         advance(0, 0, j)
+        if j == 1:
+            for h in range(2):
+                reduce_copy(1, 1, h, 0).start()
+
+    @pl.loop(1, n)
+    def _(d):
+        exchange(d)[1].wait()
 
     hidden = hidden_ref[...].astype(jnp.float32)
     later = list(range(1, levels))
@@ -301,16 +342,20 @@
                 advance(1, 1, later.pop(0))
         units_wide = units.shape[1]
 
+        def pushed(at):
+            second = jnp.dot(
+                x_all[1][...], wgu[span:, pl.ds(at, UNIT_TILE)], preferred_element_type=jnp.float32
+            )
+            back = [to_first.index(b) for b in range(n)]
+            return jnp.dot(
+                x_all[0][...], wgu[:span, pl.ds(at, UNIT_TILE)], preferred_element_type=jnp.float32
+            ) + reordered(second, back)
+
         @pl.loop(0, units_wide // UNIT_TILE)
         def _(i):
             at = pl.multiple_of(i * UNIT_TILE, UNIT_TILE)
-            gate = jnp.dot(
-                x_all[...], wgu[:, pl.ds(at, UNIT_TILE)], preferred_element_type=jnp.float32
-            )
-            up_at = pl.multiple_of(units_wide + i * UNIT_TILE, UNIT_TILE)
-            up = jnp.dot(
-                x_all[...], wgu[:, pl.ds(up_at, UNIT_TILE)], preferred_element_type=jnp.float32
-            )
+            gate = pushed(at)
+            up = pushed(pl.multiple_of(units_wide + i * UNIT_TILE, UNIT_TILE))
             units[:, pl.ds(at, UNIT_TILE)] = (gate / (1.0 + jnp.exp(-gate)) * up).astype(
                 jnp.bfloat16
             )
@@ -321,16 +366,22 @@
                 advance(1, 1, later.pop(0))
 
         share = share_all[:, tick * rows : (tick + 1) * rows, :].reshape(n * rows, 128)[:, :1]
-
-        @pl.loop(0, width // TILE)
-        def _(i):
-            at = pl.ds(pl.multiple_of(i * TILE, TILE), TILE)
-            keep_and_send(
-                0, jnp.dot(units[...], wd[:, at], preferred_element_type=jnp.float32) * share, at
-            )
-
         call = 2 + tick
-        reduce_copy(0, call, 0).start()
+        for h in range(2):
+
+            @pl.loop(0, span // TILE)
+            def _(i):
+                at = pl.ds(pl.multiple_of(i * TILE, TILE), TILE)
+                down = wd[:, pl.ds(pl.multiple_of(h * span + i * TILE, TILE), TILE)]
+                keep_and_send(
+                    0,
+                    h,
+                    jnp.dot(units[...], down, preferred_element_type=jnp.float32) * share,
+                    at,
+                )
+
+            reduce_copy(0, call, h, 0).start()
+
         if tick == 0:
             while later:
                 advance(1, 1, later.pop(0))
@@ -360,9 +411,10 @@
     cols = proj_rows.shape[0]
     vmem, dma = pltpu.VMEM, pltpu.SemaphoreType.DMA
     bf16, f32 = jnp.bfloat16, jnp.float32
-    folded_shape = (2 * rows, width // 2)
-    halves = [vmem((n * rows >> (j + 1), width), bf16) for j in range(levels - 1)]
-    halves.append(vmem(folded_shape, bf16))
+    span = width // 2
+    h_shape, x_shape = (2 * rows, span), (2 * rows, span // 2)
+    halves = [vmem((n * rows >> (j + 1), span), bf16) for j in range(levels - 1)]
+    halves.append(vmem(x_shape, bf16))
     return pl.pallas_call(
         functools.partial(layers_kernel, n, sections),
         out_shape=jax.ShapeDtypeStruct((rows, width), bf16),
@@ -375,15 +427,14 @@
             vmem(w_out.shape, bf16),
             vmem((n, 2 * rows, cols), bf16),
             vmem((n, 2 * rows, 128), f32),
-            vmem((n * rows, width), bf16),
             vmem((n * rows, w_out.shape[0]), bf16),
-            vmem(folded_shape, bf16),
-            vmem(folded_shape, bf16),
-            vmem(folded_shape, bf16),
-            vmem(folded_shape, bf16),
+            vmem(h_shape, bf16),
+            vmem(h_shape, bf16),
         ]
-        + [vmem((n * rows // 2, width), f32)] * 2
-        + halves * 4
+        + [vmem((n * rows, span), bf16)] * 2
+        + [vmem(x_shape, bf16)] * 4
+        + [vmem((n * rows // 2, span), f32)] * 4
+        + halves * 8
         + [
             dma((3,)),
             dma((2,)),
@@ -391,10 +442,10 @@
             dma((n,)),
             dma((n,)),
             dma((n,)),
+            dma((8, levels)),
+            dma((8, levels)),
             dma((4, levels)),
             dma((4, levels)),
-            dma((2, levels)),
-            dma((2, levels)),
             dma(()),
             dma(()),
         ],

time: 142 us -> 125 us (0.88)
  Pallas kernels: 131 us -> 115 us
    pallas_call x1, Pallas kernels: 125 us -> 108 us  [layers_all(): pl.pallas_call(functools.partial(layers_kernel, n, sections), out_shape=j...]
where the time goes in v2:
time: 125 us; the launch traced here: 124 us
  Pallas kernels  115 us (92%)
  local copies, waits for them, and re-layouts  8.03 us (6%)
  other arithmetic  1.61 us (1%)
    pallas_call x1, Pallas kernels, layers_all(): pl.pallas_call(functools.partial(layers_kernel, n, sections), out_shape=j...  108 us
    unnamed x11, local copies, waits for them, and re-layouts  7.05 us
    pallas_call x1, Pallas kernels, attend_all(): pl.pallas_call(attend_kernel, out_shape=jax.ShapeDtypeStruct((micros, row...  6.67 us

profile of v2, /device:TPU:0, one launch (start us, length us, event | category | flops | bytes accessed | tf_op | source)
XLA Modules:
  0.0 124.2 jit_solution(11560902781655469480)
XLA Ops:
  0.0 0.0 copy-start
  0.0 1.0 copy.30
  1.0 0.8 copy.31
  1.8 0.0 copy-start.1
  1.8 2.2 %copy-done.1 = bf16[1,2,8,128,1024]{4,3,2,1,0:T(8,128)(2,1)S(1)} copy-done((bf16[1,2,8,128,1024]{4,3,2,1,0:T(8,128)(2,1)S(1)}, bf16[1,2,8,128,1024]{4,3,2,1,0:T(8,128)(2,1)}, u32[]{:S(2)}) %copy-start.1) | copy-done | bytes 4194328
  4.0 0.0 copy-start.2
  4.0 0.7 copy-done.2
  4.7 6.7 %shard_map.109 = bf16[2,8,64,128]{3,2,1,0:T(8,128)(2,1)S(1)} custom-call(s32[2]{0:T(128)S(1)} %and_select_fusion.order_ref, s32[2,8]{1,0:T(2,128)S(1)} %copy-done.2, bf16[2,8,64,128]{3,2,1,0:T(8,128)(2,1)S(1)} %copy.30, bf16[2,8,8,128]{3,2,1,0:T(8,128)(2,1)S(1)} %copy.31, bf16[2,8,128,1024]{3,2,1,0:T(8,128)(2,1)S(1)} %bitcast.32), custom_call_target="tpu_custom_call" | custom-call | tf_op jit(solution)/shard_map/pallas_call | solution.py:84
  11.3 0.9 copy.29
  12.2 0.8 reduce_sum.18
  13.0 0.8 bitcast_divide_fusion
  13.8 0.1 copy.21
  13.8 0.0 copy-done
  13.8 0.1 constant_dynamic-slice_fusion
  13.9 0.1 copy.22
  14.0 0.1 copy.20
  14.1 0.8 broadcast_in_dim.28.share_ref
  14.9 107.9 %shard_map.110 = bf16[8,4096]{1,0:T(8,128)(2,1)} custom-call(bf16[16,8192]{1,0:T(8,128)(2,1)} %bitcast.36, f32[16,16,128]{2,1,0:T(8,128)} %broadcast_in_dim.28.share_ref, bf16[8,4096]{1,0:T(8,128)(2,1)} %bitcast.39, f32[1,4096]{1,0:T(1,128)} %gain_ref.1, bf16[512,4096]{1,0:T(8,128)(2,1)} %bitcast.35, bf16[4096,1536]{1,0:T(8,128)(2,1)} %bitcast.33, ...), custom_call_target="tpu_custom_call" | custom-call | flops 5905580032 | bytes 23068672 | tf_op jit(solution)/shard_map/pallas_call | solution.py:418
  122.7 1.5 %copy.33 = bf16[1,8,4096]{2,1,0:T(8,128)(2,1)} copy(bf16[1,8,4096]{2,1,0:T(8,128)(2,1)} %bitcast.37) | data formatting | bytes 131072
  (4 shorter events, 0.1 us)
Async XLA Ops:
  0.0 13.8 %copy-start = (s32[1,2,128,8]{2,3,1,0:T(8,128)S(1)}, s32[1,2,128,8]{2,3,1,0:T(8,128)}, u32[]{:S(2)}) copy-start(s32[1,2,128,8]{2,3,1,0:T(8,128)} %param.20) | copy-start | bytes 24580
  1.8 2.2 %copy-start.1 = (bf16[1,2,8,128,1024]{4,3,2,1,0:T(8,128)(2,1)S(1)}, bf16[1,2,8,128,1024]{4,3,2,1,0:T(8,128)(2,1)}, u32[]{:S(2)}) copy-start(bf16[1,2,8,128,1024]{4,3,2,1,0:T(8,128)(2,1)} %param.14) | copy-start | bytes 12582916
  4.0 0.7 copy-start.2

commit v3 on v2

--- a/solution.py
+++ b/solution.py
@@ -111,11 +111,11 @@
     return jnp.concatenate([wide[:half], wide[half:]], axis=1)
 
 
-def layers_kernel(n, sections, a_ref, share_ref, hidden_ref, gain_ref, wo_hbm, wgu_hbm, wd_hbm, out_ref, *scratch):
+def layers_kernel(n, sections, a_ref, picks_ref, weights_ref, hidden_ref, gain_ref, wo_hbm, wgu_hbm, wd_hbm, out_ref, *scratch):
     levels = n.bit_length() - 1
-    (wo, wgu, wd, a_all, share_all, units, h_out, h_in) = scratch[:8]
-    x_all, x_out, x_in = scratch[8:10], scratch[10:12], scratch[12:14]
-    rest = scratch[14:]
+    (wo, wgu, wd, a_all, share_ref, share_all, units, h_out, h_in) = scratch[:9]
+    x_all, x_out, x_in = scratch[9:11], scratch[11:13], scratch[13:15]
+    rest = scratch[15:]
     acc = (rest[:2], rest[2:4])
     rest = rest[4:]
     parts = [rest[i * levels : (i + 1) * levels] for i in range(8)]
@@ -130,7 +130,7 @@
     span = width // 2
     cols = a_all.shape[2]
     bits = [(me // (1 << j)) % 2 for j in range(levels)]
-    orders = (list(range(levels)), [0] + list(range(2, levels)) + [1])
+    orders = (list(range(levels)), [0, 2, 1] + list(range(3, levels)))
     places = [
         sum(bits[order[i]] * (1 << (levels - 1 - i)) for i in range(levels)) for order in orders
     ]
@@ -197,18 +197,28 @@
             ),
         )
 
-    for which in range(2):
-
-        @pl.loop(1, n)
-        def _(d):
-            exchange(d)[which].start()
+    @pl.loop(1, n)
+    def _(d):
+        exchange(d)[0].start()
 
     own = (
         pltpu.make_async_copy(a_part(me), a_all.at[place], own_sem.at[0]),
         pltpu.make_async_copy(share_ref.at[me], share_all.at[place], own_sem.at[1]),
     )
-    for copy in own:
-        copy.start()
+    own[0].start()
+    weights = weights_ref[...]
+    shares = weights / jnp.sum(weights, axis=-1, keepdims=True)
+    for expert in range(n):
+        named = jnp.where(picks_ref[...] == expert, shares, 0.0)
+        share_ref[expert] = jnp.broadcast_to(
+            jnp.sum(named, axis=-1, keepdims=True), share_ref.shape[1:]
+        )
+
+    @pl.loop(1, n)
+    def _(d):
+        exchange(d)[1].start()
+
+    own[1].start()
     for copy in own:
         copy.wait()
 
@@ -405,7 +415,7 @@
             out_ref[...] = done.astype(jnp.bfloat16)
 
 
-def layers_all(n, sections, attn, share, hidden, gain, proj_rows, w_pair, w_out):
+def layers_all(n, sections, attn, picks, weights, hidden, gain, proj_rows, w_pair, w_out):
     levels = n.bit_length() - 1
     rows, width = hidden.shape
     cols = proj_rows.shape[0]
@@ -418,7 +428,7 @@
     return pl.pallas_call(
         functools.partial(layers_kernel, n, sections),
         out_shape=jax.ShapeDtypeStruct((rows, width), bf16),
-        in_specs=[pl.BlockSpec(memory_space=pltpu.VMEM)] * 4
+        in_specs=[pl.BlockSpec(memory_space=pltpu.VMEM)] * 5
         + [pl.BlockSpec(memory_space=pl.ANY)] * 3,
         out_specs=pl.BlockSpec(memory_space=pltpu.VMEM),
         scratch_shapes=[
@@ -426,6 +436,7 @@
             vmem(w_pair.shape, bf16),
             vmem(w_out.shape, bf16),
             vmem((n, 2 * rows, cols), bf16),
+            vmem((n, 2 * rows, 128), f32),
             vmem((n, 2 * rows, 128), f32),
             vmem((n * rows, w_out.shape[0]), bf16),
             vmem(h_shape, bf16),
@@ -457,7 +468,7 @@
             bytes_accessed=int(2 * width * (cols + 3 * w_out.shape[0])),
             transcendentals=0,
         ),
-    )(attn, share, hidden, gain, proj_rows, w_pair, w_out)
+    )(attn, picks, weights, hidden, gain, proj_rows, w_pair, w_out)
 
 
 def on_device(
@@ -482,17 +493,15 @@
     attn = attend_all(order, lengths, query[0], new_kv[0], kv_cache[0])
     picks = lax.dynamic_slice_in_dim(expert_ids[0], member * rows, rows, 1)
     weights = route_weight[0]
-    share = weights / jnp.sum(weights, axis=-1, keepdims=True)
     swap = position == 1
     picks = jnp.where(swap, picks[::-1], picks).reshape(2 * rows, -1)
-    share = jnp.where(swap, share[::-1], share).reshape(2 * rows, -1)
-    chosen = picks[None] == jnp.arange(n, dtype=jnp.int32)[:, None, None]
-    dense = jnp.sum(jnp.where(chosen, share[None], 0.0), axis=-1)
+    weights = jnp.where(swap, weights[::-1], weights).reshape(2 * rows, -1)
     return layers_all(
         n,
         sections,
         attn.reshape(2 * rows, HEADS * HD),
-        jnp.broadcast_to(dense[:, :, None], (n, 2 * rows, 128)),
+        picks,
+        weights,
         hidden_in[0],
         norm_gain,
         out_proj[0],

time: 125 us -> 119 us (0.952)
  Pallas kernels: 115 us -> 109 us
    pallas_call x1, Pallas kernels: 108 us -> 103 us  [layers_all(): pl.pallas_call(functools.partial(layers_kernel, n, sections), out_shape=j...]
    reshape x0 -> x2, other arithmetic: none -> 1.98 us  [the longest x1 1.37 us: on_device(): weights = jnp.where(swap, weights[::-1], weights).reshape(2 * rows, -1)]
where the time goes in v3:
time: 119 us; the launch traced here: 118 us
  Pallas kernels  109 us (92%)
  local copies, waits for them, and re-layouts  7.12 us (6%)
  other arithmetic  1.99 us (2%)
    pallas_call x1, Pallas kernels, layers_all(): pl.pallas_call(functools.partial(layers_kernel, n, sections), out_shape=j...  103 us
    unnamed x11, local copies, waits for them, and re-layouts  7.05 us
    pallas_call x1, Pallas kernels, attend_all(): pl.pallas_call(attend_kernel, out_shape=jax.ShapeDtypeStruct((micros, row...  6.67 us

profile of v3, /device:TPU:0, one launch (start us, length us, event | category | flops | bytes accessed | tf_op | source)
XLA Modules:
  0.0 118.4 jit_solution(15341524588923845827)
XLA Ops:
  0.0 0.0 copy-start
  0.0 1.0 copy.27
  1.0 0.8 copy.28
  1.8 0.0 copy-start.1
  1.8 2.2 %copy-done.1 = bf16[1,2,8,128,1024]{4,3,2,1,0:T(8,128)(2,1)S(1)} copy-done((bf16[1,2,8,128,1024]{4,3,2,1,0:T(8,128)(2,1)S(1)}, bf16[1,2,8,128,1024]{4,3,2,1,0:T(8,128)(2,1)}, u32[]{:S(2)}) %copy-start.1) | copy-done | bytes 4194328
  4.0 0.0 copy-start.2
  4.0 0.7 copy-done.2
  4.7 6.7 %shard_map.109 = bf16[2,8,64,128]{3,2,1,0:T(8,128)(2,1)S(1)} custom-call(s32[2]{0:T(128)S(1)} %and_select_fusion.order_ref, s32[2,8]{1,0:T(2,128)S(1)} %copy-done.2, bf16[2,8,64,128]{3,2,1,0:T(8,128)(2,1)S(1)} %copy.27, bf16[2,8,8,128]{3,2,1,0:T(8,128)(2,1)S(1)} %copy.28, bf16[2,8,128,1024]{3,2,1,0:T(8,128)(2,1)S(1)} %bitcast.31), custom_call_target="tpu_custom_call" | custom-call | tf_op jit(solution)/shard_map/pallas_call | solution.py:84
  11.3 0.9 copy.26
  12.2 0.0 copy-done
  12.2 0.1 constant_dynamic-slice_fusion
  12.3 0.1 copy.19
  12.3 0.6 fusion.picks_ref
  12.9 1.4 %fusion.1.weights_ref = f32[16,8]{1,0:T(8,128)} fusion(f32[2,8,8]{2,1,0:T(8,128)} %bitcast.41, pred[]{:T(512)S(6)} %eq.5), kind=kLoop, calls=%fused_computation.6 | loop fusion | flops 128 | bytes 1025 | tf_op jit(solution)/shard_map/reshape | solution.py:498
  14.3 102.6 %shard_map.110 = bf16[8,4096]{1,0:T(8,128)(2,1)} custom-call(bf16[16,8192]{1,0:T(8,128)(2,1)} %bitcast.35, s32[16,8]{1,0:T(8,128)} %fusion.picks_ref, f32[16,8]{1,0:T(8,128)} %fusion.1.weights_ref, bf16[8,4096]{1,0:T(8,128)(2,1)} %bitcast.38, f32[1,4096]{1,0:T(1,128)} %gain_ref.1, bf16[512,4096]{1,0:T(8,128)(2,1)} %bitcast.34, bf16[4096,1536]{1,0:T(8,128)(2,1)} %bitcast.32, ...), custom_call_target="tpu_custom_call" | custom-call | flops 5905580032 | bytes 23068672 | tf_op jit(solution)/shard_map/pallas_call | solution.py:428
  116.9 1.5 %copy.30 = bf16[1,8,4096]{2,1,0:T(8,128)(2,1)} copy(bf16[1,8,4096]{2,1,0:T(8,128)(2,1)} %bitcast.36) | data formatting | bytes 131072
  (1 shorter events, 0.0 us)
Async XLA Ops:
  0.0 12.2 %copy-start = (s32[1,2,128,8]{2,3,1,0:T(8,128)S(1)}, s32[1,2,128,8]{2,3,1,0:T(8,128)}, u32[]{:S(2)}) copy-start(s32[1,2,128,8]{2,3,1,0:T(8,128)} %param.20) | copy-start | bytes 24580
  1.8 2.2 %copy-start.1 = (bf16[1,2,8,128,1024]{4,3,2,1,0:T(8,128)(2,1)S(1)}, bf16[1,2,8,128,1024]{4,3,2,1,0:T(8,128)(2,1)}, u32[]{:S(2)}) copy-start(bf16[1,2,8,128,1024]{4,3,2,1,0:T(8,128)(2,1)} %param.14) | copy-start | bytes 12582916
  4.0 0.7 copy-start.2
